TPU v7x, 512 devices: a whole 4x4x16 slice. The times are simulated.
512 devices in a mesh: view: 16 (over z), head: 32 (over y, x, core).
Axes of the slice: x: 4, y: 4, z: 16, core: 2. Of those that a mesh axis runs over, the one named last changes fastest.
Arguments:
- queries: bfloat16 [32768, 4096], P('view', 'head'), may hold values from -6 to 6
- key_tokens: bfloat16 [32768, 4096], P('view', 'head'), may hold values from -6 to 6
- value_tokens: bfloat16 [32768, 4096], P('view', 'head'), may hold values from -64 to 64
- block_lists: int32 [512, 4], P('view'), may hold values from -1 to 479, as said below
- gain_soft: float32 [4096], P('head'), may hold values from 0.25 to 1.75
- gain_linear: float32 [4096], P('head'), may hold values from 0.25 to 1.75
Outputs:
- layer_out: bfloat16 [32768, 4096], P('view', 'head')
Inputs may be any that keep to these rules, and one draw needn't show every extreme that they name: `block_lists`: rows of the first view are all -1. Each row of a later view v lists 4 distinct blocks, all in views before v; the rows of view v together list exactly 4 distinct blocks of each earlier view.
All inputs are finite; a program needn't handle non-finite values.
Results may differ from a plain program's by a relative error of at most 0.0038.
Values may be sent and summed in bfloat16 or wider, within the bound.
A program may use at most 64 MiB of HBM per device.

v0:
```python
import jax
import jax.numpy as jnp
from jax import lax
from jax.sharding import PartitionSpec as P

HEAD_DIM = 128
BLOCK = 64
TOPK = 4


norm_eps = 1e-06


def entering(array, axis, combine, identity):
    devices, place = (lax.axis_size(axis), lax.axis_index(axis))
    everything = lax.all_gather(array.astype(jnp.bfloat16), axis)
    start = jnp.broadcast_to(jnp.asarray(identity, array.dtype), array.shape)

    def turn(k, before):
        reached = k < place
        new = combine(before, everything[k].astype(array.dtype))
        return jnp.where(reached, new, before)

    return lax.fori_loop(0, devices, turn, start)


def feature(values_in):
    return jax.nn.elu(values_in) + 1.0


def add_states(earlier, later):
    return earlier + later


def shards(queries, key_tokens, value_tokens, block_lists, gain_soft, gain_linear):
    row_count, columns = queries.shape
    heads = columns // HEAD_DIM
    blocks_here = row_count // BLOCK
    score_scale = HEAD_DIM ** (-0.5)
    query_heads = queries.reshape(row_count, heads, HEAD_DIM)
    key_heads = key_tokens.reshape(row_count, heads, HEAD_DIM)
    value_heads = value_tokens.reshape(row_count, heads, HEAD_DIM)
    states = jnp.einsum(
        "thd,the->hde",
        feature(key_heads.astype(jnp.float32)),
        value_heads.astype(jnp.float32),
        precision=lax.Precision.HIGHEST,
    )
    prefix = entering(states, "view", add_states, jnp.zeros_like(states))
    listed = block_lists >= 0
    empty_blocks = jnp.zeros((blocks_here, TOPK, BLOCK, columns), jnp.bfloat16)
    pieces = (
        lax.all_gather(key_tokens, "view", axis=0, tiled=True),
        lax.all_gather(value_tokens, "view", axis=0, tiled=True),
    )
    piece_blocks = pieces[0].shape[0] // BLOCK
    within = (block_lists >= 0) & (block_lists < piece_blocks) & listed
    position = jnp.clip(block_lists, 0, piece_blocks - 1)
    key_rows = jnp.take(pieces[0].reshape(piece_blocks, BLOCK, columns), position, axis=0)
    value_rows = jnp.take(pieces[1].reshape(piece_blocks, BLOCK, columns), position, axis=0)
    chosen = within[:, :, None, None]
    listed_keys = jnp.where(chosen, key_rows, empty_blocks)
    listed_values = jnp.where(chosen, value_rows, empty_blocks)
    row_span = min(512, row_count)
    block_count = row_span // BLOCK
    span_count = row_count // row_span
    key_listed = listed_keys.reshape(span_count, block_count, TOPK * BLOCK, heads, HEAD_DIM)
    value_listed = listed_values.reshape(span_count, block_count, TOPK * BLOCK, heads, HEAD_DIM)
    mask_rows = jnp.repeat(listed, BLOCK, axis=1).reshape(span_count, block_count, TOPK * BLOCK)

    def row_block(block_inputs):
        query_rows, key_block, value_block, remote_mask, row_start = block_inputs
        local_scores = (
            jnp.einsum("rhd,thd->hrt", query_rows, key_heads, preferred_element_type=jnp.float32)
            * score_scale
        )
        causal = (row_start + jnp.arange(row_span))[:, None] >= jnp.arange(row_count)[None, :]
        local_scores = jnp.where(causal[None], local_scores, -jnp.inf)
        query_blocks = query_rows.reshape(block_count, BLOCK, heads, HEAD_DIM)
        remote_scores = (
            jnp.einsum(
                "nbhd,nkhd->hnbk", query_blocks, key_block, preferred_element_type=jnp.float32
            )
            * score_scale
        )
        remote_scores = jnp.where(remote_mask[None, :, None, :], remote_scores, -jnp.inf)
        row_max = jnp.maximum(
            jnp.max(local_scores, axis=2), jnp.max(remote_scores, axis=3).reshape(heads, row_span)
        )
        local_probs = jnp.exp(local_scores - row_max[:, :, None])
        remote_probs = jnp.exp(
            remote_scores - row_max.reshape(heads, block_count, BLOCK)[:, :, :, None]
        )
        row_total = jnp.sum(local_probs, axis=2) + jnp.sum(remote_probs, axis=3).reshape(
            heads, row_span
        )
        local_weights = local_probs.astype(jnp.bfloat16)
        remote_weights = remote_probs.astype(jnp.bfloat16)
        weighted = jnp.einsum(
            "hrt,thd->rhd", local_weights, value_heads, preferred_element_type=jnp.float32
        )
        weighted = weighted + jnp.einsum(
            "hnbk,nkhd->nbhd", remote_weights, value_block, preferred_element_type=jnp.float32
        ).reshape(row_span, heads, HEAD_DIM)
        attended = weighted / row_total.T[:, :, None]
        query_feat = feature(query_rows.astype(jnp.float32))
        linear = jnp.einsum("rhd,hde->rhe", query_feat, prefix, precision=lax.Precision.HIGHEST)
        weight = jnp.einsum(
            "nbhd,nkhd->hnbk",
            query_feat.reshape(block_count, BLOCK, heads, HEAD_DIM),
            feature(key_block.astype(jnp.float32)),
            precision=lax.Precision.HIGHEST,
        )
        weight = weight * remote_mask[None, :, None, :].astype(jnp.float32)
        correction = jnp.einsum(
            "hnbk,nkhe->nbhe",
            weight,
            value_block.astype(jnp.float32),
            precision=lax.Precision.HIGHEST,
        ).reshape(row_span, heads, HEAD_DIM)
        return (attended, linear - correction)

    attended, linear = lax.map(
        row_block,
        (
            query_heads.reshape(span_count, row_span, heads, HEAD_DIM),
            key_listed,
            value_listed,
            mask_rows,
            jnp.arange(span_count) * row_span,
        ),
    )
    attended = attended.reshape(row_count, heads, HEAD_DIM)
    linear = linear.reshape(row_count, heads, HEAD_DIM)
    soft_squares, linear_squares = lax.psum(
        (jnp.sum(attended * attended, axis=(1, 2)), jnp.sum(linear * linear, axis=(1, 2))), "head"
    )
    full_width = heads * lax.axis_size("head") * HEAD_DIM
    soft_scale = lax.rsqrt(soft_squares / full_width + norm_eps)
    linear_scale = lax.rsqrt(linear_squares / full_width + norm_eps)
    layer_out = attended * soft_scale[:, None, None] * gain_soft.reshape(
        heads, HEAD_DIM
    ) + linear * linear_scale[:, None, None] * gain_linear.reshape(heads, HEAD_DIM)
    return layer_out.reshape(row_count, columns).astype(jnp.bfloat16)


def solution(mesh):
    in_specs = (
        P("view", "head"),
        P("view", "head"),
        P("view", "head"),
        P("view", None),
        P("head"),
        P("head"),
    )
    out_specs = P("view", "head")
    return jax.shard_map(shards, mesh=mesh, in_specs=in_specs, out_specs=out_specs, check_vma=False)
```

profile of v0, /device:TPU:480, one launch (start us, length us, event | category | flops | bytes accessed | tf_op | source)
XLA Modules:
  0.0 438.6 jit_solution(13906545493712832062)
XLA Ops:
  6.5 0.7 all-gather.4.cloned.1.call-update
  7.3 0.7 all-gather.6.cloned.1.call-update
  8.0 0.7 and_and_fusion
  8.9 0.7 compare_select_fusion.8
  10.2 2.5 convolution_convert_fusion
  12.7 31.7 %all-gather = bf16[2048,128]{1,0:T(8,128)(2,1)S(1)} all-gather(bf16[128,128]{1,0:T(8,128)(2,1)S(1)} %convolution_convert_fusion), channel_id=2, replica_groups=mesh['view'=16,'head'=32] {'view'}, dimensions={0}, use_global_device_ids=true | all-gather | bytes 557056 | tf_op jit(solution)/shard_map/all_gather | solution.py:16
  44.4 0.7 while.27
  45.1 69.6 %all-gather.4.cloned.1.call-done = bf16[32768,128]{1,0:T(8,128)(2,1)} async-done(((bf16[2048,128]{1,0:T(8,128)(2,1)}), bf16[32768,128]{1,0:T(8,128)(2,1)}) %all-gather.4.cloned.1.call-update) | async-done | bytes 8388624 | tf_op jit(solution)/shard_map/all_gather | solution.py:53
  114.7 5.5 %gather_fusion = bf16[128,64,128]{2,1,0:T(8,128)(2,1)} fusion(bf16[512,64,128]{2,1,0:T(8,128)(2,1)} %bitcast.169, s32[1024]{0:T(1024)S(1)} %pad_clamp_fusion), kind=kCustom, calls=%fused_computation.clone | custom fusion | bytes 4194816 | tf_op jit(solution)/shard_map/jit(_take)/gather | solution.py:59
  120.2 100.2 %all-gather.6.cloned.1.call-done = bf16[32768,128]{1,0:T(8,128)(2,1)} async-done(((bf16[2048,128]{1,0:T(8,128)(2,1)}), bf16[32768,128]{1,0:T(8,128)(2,1)}) %all-gather.6.cloned.1.call-update) | async-done | bytes 8388624 | tf_op jit(solution)/shard_map/all_gather | solution.py:54
  220.4 5.6 %gather_fusion.1 = bf16[128,64,128]{2,1,0:T(8,128)(2,1)} fusion(bf16[512,64,128]{2,1,0:T(8,128)(2,1)} %bitcast.170, s32[1024]{0:T(1024)S(1)} %pad_clamp_fusion), kind=kCustom, calls=%fused_computation.1.clone | custom fusion | bytes 4194816 | tf_op jit(solution)/shard_map/jit(_take)/gather | solution.py:60
  226.0 3.6 select_select_fusion
  229.6 69.4 %while.26 = (s32[]{:T(128)}, f32[4,512,1,128]{3,1,2,0:T(8,128)}, f32[4,512,1,128]{3,1,2,0:T(8,128)}, s32[4]{0:T(128)S(1)}, bf16[4,512,1,128]{3,1,2,0:T(8,128)(2,...) while((s32[]{:T(128)}, f32[4,512,1,128]{3,1,2,0:T(8,128)}, ...), condition=%wide.region_7.9_spmd, body=%wide.region_2.8_spmd.sunk | while | flops 1118898176 | bytes 37632176 | solution.py:123
  229.6 0.9 constant_dynamic-slice_fusion.2
  230.5 1.4 fusion.115
  232.6 0.7 iota_add_fusion.2
  233.3 3.8 fusion.116
  237.6 3.0 fusion.118
  241.1 1.5 fusion.120
  242.6 2.7 convolution_multiply_fusion.3
  245.8 1.2 fusion.122
  246.9 0.9 constant_dynamic-slice_fusion.2
  247.9 1.4 fusion.115
  250.0 0.7 iota_add_fusion.2
  250.7 3.8 fusion.116
  255.0 3.0 fusion.118
  258.5 1.5 fusion.120
  260.0 2.7 convolution_multiply_fusion.3
  263.1 1.1 fusion.122
  264.3 0.9 constant_dynamic-slice_fusion.2
  265.2 1.4 fusion.115
  267.3 0.7 iota_add_fusion.2
  268.0 3.8 fusion.116
  272.3 3.0 fusion.118
  275.8 1.5 fusion.120
  277.3 2.7 convolution_multiply_fusion.3
  280.5 1.1 fusion.122
  281.6 0.9 constant_dynamic-slice_fusion.2
  282.5 1.4 fusion.115
  284.6 0.7 iota_add_fusion.2
  285.3 3.8 fusion.116
  289.7 3.0 fusion.118
  293.1 1.5 fusion.120
  294.7 2.7 convolution_multiply_fusion.3
  297.8 1.1 fusion.122
  299.0 2.2 multiply_reduce_fusion
  301.2 128.1 %all-reduce = (f32[2048]{0:T(1024)S(1)}, f32[2048]{0:T(1024)S(1)}) all-reduce(f32[2048]{0:T(1024)S(1)} %bitcast.175, f32[2048]{0:T(1024)S(1)} %bitcast.174), channel_id=1, replica_groups=mesh['view'=16,'head'=32] {'head'}, use_global_device_ids=true, to_apply=%region_11.13 | all-reduce | flops 4096 | bytes 32768 | tf_op jit(solution)/shard_map/psum | solution.py:135
  429.3 2.5 fusion.71
  (94 shorter events, 9.0 us)
Async XLA Ops:
  6.5 108.2 %all-gather.4.cloned.1.call-start = ((), (), s32[]{:S(2)}) async-start(), calls=%async_computation | async-start | bytes 8912896 | tf_op jit(solution)/shard_map/all_gather | solution.py:53
  7.3 213.1 %all-gather.6.cloned.1.call-start = ((), (), s32[]{:S(2)}) async-start(), calls=%async_computation.1 | async-start | bytes 8912896 | tf_op jit(solution)/shard_map/all_gather | solution.py:54
  226.0 3.6 copy-start.1
  237.6 3.5 copy-start
  255.0 3.5 copy-start
  272.3 3.5 copy-start
  289.7 3.5 copy-start
  299.0 130.4 %copy-start.2 = (f32[4,512,1,128]{3,1,2,0:T(8,128)S(1)}, f32[4,512,1,128]{3,1,2,0:T(8,128)}, u32[]{:S(2)}) copy-start(f32[4,512,1,128]{3,1,2,0:T(8,128)} %get-tuple-element.144) | copy-start | bytes 3145732
  299.0 130.4 %copy-start.3 = (f32[128]{0:T(128)S(1)}, f32[128]{0:T(128)}, u32[]{:S(2)}) copy-start(f32[128]{0:T(128)} %param.17) | copy-start | bytes 1540
  299.0 130.4 %copy-start.4 = (f32[128]{0:T(128)S(1)}, f32[128]{0:T(128)}, u32[]{:S(2)}) copy-start(f32[128]{0:T(128)} %param.16) | copy-start | bytes 1540
Sparse Core Ops, SparseCore 0:
  9.4 105.2 all-gather.3
  116.8 103.5 all-gather.5
where the time goes:
time: 445 us; the launch traced here: 439 us
  waiting for transfers between devices  171 us (38%)
  blocking collectives  160 us (36%)
  matrix products  47.9 us (11%)
  other arithmetic  26 us (6%)
  local copies, waits for them, and re-layouts  19.6 us (4%)
  between operations  13.5 us (3%)
    psum x1, blocking collectives, shards(): lax.psum((jnp.sum(attended * attended, axis=(1, 2)), jnp.sum(linear * lin...  128 us
    all_gather x1, waiting for transfers between devices, shards(): lax.all_gather(value_tokens, 'view', axis=0, tiled=True)  100 us
    all_gather x1, waiting for transfers between devices, shards(): lax.all_gather(key_tokens, 'view', axis=0, tiled=True)  69.6 us
    all_gather x1, blocking collectives, entering(): everything = lax.all_gather(array.astype(jnp.bfloat16), axis)  31.7 us
    dot_general x4, matrix products, row_block(): jnp.einsum('rhd,thd->hrt', query_rows, key_heads, preferred_element_type=...  15.3 us
    reduce_sum x4, other arithmetic, row_block(): jnp.sum(local_probs, axis=2)  12.1 us
    dot_general x4, matrix products, row_block(): jnp.einsum('nbhd,nkhd->hnbk', query_feat.reshape(block_count, BLOCK, head...  11 us
  transfers between devices with their start and end apart: 2, of which 2 were waited for; matrix products, arithmetic and copies ran while one was open for 2% of the time, Pallas kernels for 0%

commit v1 on v0

v1 whole, which is shorter than its diff:
```python
import functools

import jax
import jax.numpy as jnp
from jax import lax
from jax.experimental import pallas as pl
from jax.experimental.pallas import tpu as pltpu
from jax.sharding import PartitionSpec as P

HEAD_DIM = 128
BLOCK = 64
TOPK = 4
CAP = 4
EPS = 1e-06
SPLITS = (2, 4, 4)
MESH = pl.DeviceIdType.MESH
NT = (((1,), (1,)), ((), ()))
TN = (((0,), (0,)), ((), ()))
HIGHEST = lax.Precision.HIGHEST


def feature(x):
    return jnp.where(x > 0, x + 1.0, jnp.exp(jnp.minimum(x, 0.0)))


def matmul(a, b):
    return jnp.dot(a, b, preferred_element_type=jnp.float32)


def matmul_nt(a, b, precision=None):
    return lax.dot_general(a, b, NT, precision=precision, preferred_element_type=jnp.float32)


def matmul_tn(a, b, precision=None):
    return lax.dot_general(a, b, TN, precision=precision, preferred_element_type=jnp.float32)


def send_order(views):
    half = views // 2
    low, high = list(range(half, views)), []
    while low:
        high.append(low.pop())
        if low:
            high.append(low.pop(0))
    return high + list(range(half - 1, 0, -1))


def kernel(
    views, heads, splits, rows,
    q_ref, k_ref, v_ref, plan_ref, pos_ref, gain_s_ref, gain_l_ref, out_ref,
    plans, plan_smem, stage, recv, states, entering, leaving, own_state,
    acc, top, total, att, lin, sums, sums_in,
    plan_send, plan_recv, bulk_send, bulk_recv, chain_sem, local_sem, sum_send, sum_recv,
):
    me = lax.axis_index("view")
    head = lax.axis_index("head")
    scale2 = 1.4426950408889634 * HEAD_DIM ** (-0.5)
    qtile = min(256, rows)
    qblocks = rows // BLOCK

    phases = []
    stride = 1
    for size in splits:
        place = head // stride % size
        phases.append([head + ((place + t) % size - place) * stride for t in range(1, size)])
        stride *= size

    barrier = pltpu.get_barrier_semaphore()
    for d in range(1, views):
        pl.semaphore_signal(
            barrier, inc=1, device_id=((me + d) % views, head), device_id_type=MESH
        )
    for partners in phases:
        for other in partners:
            pl.semaphore_signal(barrier, inc=1, device_id=(me, other), device_id_type=MESH)
    pl.semaphore_wait(barrier, views - 1 + sum(len(p) for p in phases))

    def plan_copy(slot, to):
        return pltpu.make_async_remote_copy(
            src_ref=plan_ref.at[to],
            dst_ref=plans.at[slot],
            send_sem=plan_send.at[to],
            recv_sem=plan_recv.at[slot],
            device_id=(to, head),
            device_id_type=MESH,
        )

    for u in range(views - 1):
        @pl.when(u < me)
        def _():
            plan_copy(me, u).start()

    own_state[...] = matmul_tn(
        feature(k_ref[...].reshape(rows, HEAD_DIM).astype(jnp.float32)).astype(jnp.bfloat16),
        v_ref[...].reshape(rows, HEAD_DIM),
    )

    def chain_copy():
        return pltpu.make_async_remote_copy(
            src_ref=leaving,
            dst_ref=entering,
            send_sem=chain_sem.at[0],
            recv_sem=chain_sem.at[1],
            device_id=((me + 1) % views, head),
            device_id_type=MESH,
        )

    @pl.when(me == 0)
    def _():
        leaving[...] = own_state[...]
        chain_copy().start()

    for w in range(1, views):
        @pl.when(w > me)
        def _():
            plan_copy(w, w).wait_recv()

    smem_copy = pltpu.make_async_copy(plans, plan_smem, local_sem)
    smem_copy.start()
    smem_copy.wait()

    def bulk_copy(slot, to):
        return pltpu.make_async_remote_copy(
            src_ref=stage.at[pl.ds(to * CAP, CAP)],
            dst_ref=recv.at[pl.ds(slot * CAP, CAP)],
            send_sem=bulk_send.at[to],
            recv_sem=bulk_recv.at[slot],
            device_id=(to, head),
            device_id_type=MESH,
        )

    for w in send_order(views):
        @pl.when(w > me)
        def _():
            for s in range(CAP):
                block = plan_smem[w, 0, s]
                stage[w * CAP + s, 0] = k_ref[block]
                stage[w * CAP + s, 1] = v_ref[block]
            bulk_copy(me, w).start()

    @pl.when(me > 0)
    def _():
        chain_copy().wait_recv()

        @pl.when(me < views - 1)
        def _():
            leaving[...] = entering[...] + own_state[...]
            chain_copy().start()

    row = lax.broadcasted_iota(jnp.int32, (qtile, qtile), 0)
    col = lax.broadcasted_iota(jnp.int32, (qtile, qtile), 1)

    per_tile = qtile // BLOCK

    def tile_of(ref, j):
        return ref[pl.ds(j * per_tile, per_tile)].reshape(qtile, HEAD_DIM)

    @pl.loop(0, rows // qtile)
    def _(i):
        mine = pl.ds(pl.multiple_of(i * qtile, qtile), qtile)
        q = q_ref[mine, :]
        s = jnp.where(row >= col, matmul_nt(q, tile_of(k_ref, i)), -jnp.inf)
        m = jnp.max(s, axis=1, keepdims=True)
        p = jnp.exp2((s - m) * scale2)
        l = jnp.sum(p, axis=1, keepdims=True)
        o = matmul(p.astype(jnp.bfloat16), tile_of(v_ref, i))

        def step(j, carry):
            m, l, o = carry
            s = matmul_nt(q, tile_of(k_ref, j))
            new = jnp.maximum(m, jnp.max(s, axis=1, keepdims=True))
            p = jnp.exp2((s - new) * scale2)
            fade = jnp.exp2((m - new) * scale2)
            l = l * fade + jnp.sum(p, axis=1, keepdims=True)
            o = o * fade + matmul(p.astype(jnp.bfloat16), tile_of(v_ref, j))
            return new, l, o

        m, l, o = lax.fori_loop(0, i, step, (m, l, o))
        acc[mine, :] = o
        top[mine, :] = jnp.broadcast_to(m, (qtile, HEAD_DIM))
        total[mine, :] = jnp.broadcast_to(l, (qtile, HEAD_DIM))

    @pl.loop(0, me)
    def _(u):
        bulk_copy(u, u).wait_recv()
        for s in range(CAP):
            states[u * CAP + s] = matmul_tn(
                feature(recv[u * CAP + s, 0].astype(jnp.float32)).astype(jnp.bfloat16),
                recv[u * CAP + s, 1],
            )

    @pl.when(me == 0)
    def _():
        att[...] = acc[...] / total[...]
        lin[...] = jnp.zeros_like(lin)

    @pl.when(me > 0)
    def _():
        @pl.loop(0, qblocks)
        def _(r):
            mine = pl.ds(pl.multiple_of(r * BLOCK, BLOCK), BLOCK)
            q = q_ref[mine, :]
            scores, values = [], []
            remaining = entering[...]
            for c in range(TOPK):
                at = pos_ref[r * TOPK + c]
                scores.append(matmul_nt(q, recv[at, 0]))
                values.append(recv[at, 1])
                remaining = remaining - states[at]
            s = jnp.concatenate(scores, axis=1)
            m_old = top[mine, :][:, :1]
            m = jnp.maximum(m_old, jnp.max(s, axis=1, keepdims=True))
            p = jnp.exp2((s - m) * scale2)
            fade = jnp.exp2((m_old - m) * scale2)
            l = total[mine, :][:, :1] * fade + jnp.sum(p, axis=1, keepdims=True)
            o = acc[mine, :] * fade + matmul(
                p.astype(jnp.bfloat16), jnp.concatenate(values, axis=0)
            )
            att[mine, :] = o / l
            qf = feature(q.astype(jnp.float32)).astype(jnp.bfloat16)
            coarse = remaining.astype(jnp.bfloat16)
            fine = (remaining - coarse.astype(jnp.float32)).astype(jnp.bfloat16)
            lin[mine, :] = matmul(qf, coarse) + matmul(qf, fine)

    parts = 4
    seg = rows // parts
    sub = lax.broadcasted_iota(jnp.int32, (2 * parts, HEAD_DIM), 0)

    def pick(i):
        return jnp.where(sub == i, 1.0, 0.0).astype(jnp.float32)

    partial = jnp.zeros((2 * parts, seg), jnp.float32)
    for t in range(parts):
        a = att[t * seg : (t + 1) * seg, :]
        b = lin[t * seg : (t + 1) * seg, :]
        partial = partial + matmul_nt(pick(2 * t), a * a, HIGHEST)
        partial = partial + matmul_nt(pick(2 * t + 1), b * b, HIGHEST)

    count = 0
    copies = []
    for phase, partners in enumerate(phases):
        sums[phase] = partial
        here = []
        for other in partners:
            copy = pltpu.make_async_remote_copy(
                src_ref=sums.at[phase],
                dst_ref=sums_in.at[count],
                send_sem=sum_send.at[count],
                recv_sem=sum_recv.at[count],
                device_id=(me, other),
                device_id_type=MESH,
            )
            copy.start()
            here.append((copy, count))
            count += 1
        for copy, at in here:
            copy.wait_recv()
            partial = partial + sums_in[at]
        copies += [copy for copy, _ in here]

    scales = lax.rsqrt(partial / (heads * HEAD_DIM) + EPS)
    gain_s, gain_l = gain_s_ref[...], gain_l_ref[...]
    for t in range(parts):
        span = slice(t * seg, (t + 1) * seg)
        soft = matmul_tn(scales, pick(2 * t), HIGHEST)
        linear = matmul_tn(scales, pick(2 * t + 1), HIGHEST)
        out_ref[span, :] = (
            att[span, :] * soft * gain_s + lin[span, :] * linear * gain_l
        ).astype(jnp.bfloat16)

    for copy in copies:
        copy.wait_send()
    for u in range(views - 1):
        @pl.when(u < me)
        def _():
            plan_copy(me, u).wait_send()
    for w in range(1, views):
        @pl.when(w > me)
        def _():
            bulk_copy(me, w).wait_send()

    @pl.when(me < views - 1)
    def _():
        chain_copy().wait_send()


def shards(views, heads, splits, q, k, v, lists, gain_s, gain_l):
    rows = q.shape[0]
    per_view = rows // BLOCK
    blocks = views * per_view
    flat = lists.reshape(-1)
    ids = jnp.arange(blocks, dtype=jnp.int32)
    present = jnp.any(flat[:, None] == ids[None, :], axis=0)
    table = present.reshape(views, per_view)
    within = jnp.arange(per_view, dtype=jnp.int32)
    earlier = within[None, :] < within[:, None]
    rank = jnp.sum(table[:, None, :] & earlier[None], axis=2, dtype=jnp.int32)
    slots = jnp.arange(HEAD_DIM, dtype=jnp.int32)
    chosen = table[:, None, :] & (rank[:, None, :] == slots[None, :, None])
    plan = jnp.sum(jnp.where(chosen, within[None, None, :], 0), axis=2, dtype=jnp.int32)
    place = (jnp.arange(views, dtype=jnp.int32)[:, None] * CAP + rank).reshape(-1)
    pos = jnp.sum(jnp.where(flat[:, None] == ids[None, :], place[None, :], 0), axis=1)

    phases = len(splits)
    partners = sum(s - 1 for s in splits)
    f32, bf16 = jnp.float32, jnp.bfloat16
    vmem = pl.BlockSpec(memory_space=pltpu.VMEM)
    smem = pl.BlockSpec(memory_space=pltpu.SMEM)
    dma = pltpu.SemaphoreType.DMA
    sums = (8, rows // 4)
    return pl.pallas_call(
        functools.partial(kernel, views, heads, splits, rows),
        out_shape=jax.ShapeDtypeStruct(q.shape, bf16),
        in_specs=[vmem, vmem, vmem, vmem, smem, vmem, vmem],
        out_specs=vmem,
        scratch_shapes=[
            pltpu.VMEM((views, 1, HEAD_DIM), jnp.int32),
            pltpu.SMEM((views, 1, HEAD_DIM), jnp.int32),
            pltpu.VMEM((views * CAP, 2, BLOCK, HEAD_DIM), bf16),
            pltpu.VMEM((views * CAP, 2, BLOCK, HEAD_DIM), bf16),
            pltpu.VMEM((views * CAP, HEAD_DIM, HEAD_DIM), f32),
            pltpu.VMEM((HEAD_DIM, HEAD_DIM), f32),
            pltpu.VMEM((HEAD_DIM, HEAD_DIM), f32),
            pltpu.VMEM((HEAD_DIM, HEAD_DIM), f32),
            pltpu.VMEM((rows, HEAD_DIM), f32),
            pltpu.VMEM((rows, HEAD_DIM), f32),
            pltpu.VMEM((rows, HEAD_DIM), f32),
            pltpu.VMEM((rows, HEAD_DIM), f32),
            pltpu.VMEM((rows, HEAD_DIM), f32),
            pltpu.VMEM((phases,) + sums, f32),
            pltpu.VMEM((partners,) + sums, f32),
            dma((views,)),
            dma((views,)),
            dma((views,)),
            dma((views,)),
            dma((2,)),
            dma,
            dma((partners,)),
            dma((partners,)),
        ],
        compiler_params=pltpu.CompilerParams(
            collective_id=0, has_side_effects=True, vmem_limit_bytes=48 * 1024 * 1024
        ),
    )(
        q,
        k.reshape(per_view, BLOCK, HEAD_DIM),
        v.reshape(per_view, BLOCK, HEAD_DIM),
        plan.reshape(views, 1, HEAD_DIM),
        pos,
        gain_s[None],
        gain_l[None],
    )


def solution(mesh, splits=SPLITS):
    views, heads = mesh.shape["view"], mesh.shape["head"]
    in_specs = (
        P("view", "head"),
        P("view", "head"),
        P("view", "head"),
        P("view", None),
        P("head"),
        P("head"),
    )
    return jax.shard_map(
        functools.partial(shards, views, heads, splits),
        mesh=mesh,
        in_specs=in_specs,
        out_specs=P("view", "head"),
        check_vma=False,
    )
```

time: 445 us -> 192 us (0.43); the launches traced: 439 us -> 191 us
  Pallas kernels: 0 us -> 185 us
  waiting for transfers between devices: 171 us -> 0 us
  blocking collectives: 160 us -> 0 us
  matrix products: 47.9 us -> 0 us
  other arithmetic: 26 us -> 0.96 us
  local copies, waits for them, and re-layouts: 19.6 us -> 5.61 us
  between operations: 13.5 us -> 0.06 us
    pallas_call x0 -> x1, Pallas kernels: none -> 185 us  [shards(): pl.pallas_call(functools.partial(kernel, views, heads, splits, rows), out...]
    all_gather x2 -> x0, waiting for transfers between devices: 170 us -> none  [the longest x1 100 us: shards(): lax.all_gather(value_tokens, 'view', axis=0, tiled=True)]
    psum x1 -> x0, blocking collectives: 128 us -> none  [shards(): lax.psum((jnp.sum(attended * attended, axis=(1, 2)), jnp.sum(linear * lin...]
    dot_general x29 -> x0, matrix products: 47.9 us -> none  [the longest x4 15.3 us: row_block(): jnp.einsum('rhd,thd->hrt', query_rows, key_heads, preferred_element_type=...]
    all_gather x1 -> x0, blocking collectives: 31.7 us -> none  [entering(): everything = lax.all_gather(array.astype(jnp.bfloat16), axis)]
    reduce_sum x9 -> x3, other arithmetic: 15.5 us -> 0.75 us  [the longest x1 0.36 us: shards(): rank = jnp.sum(table[:, None, :] & earlier[None], axis=2, dtype=jnp.int32)]
    gather x2 -> x0, local copies, waits for them, and re-layouts: 11.1 us -> none  [the longest x1 5.59 us: shards(): jnp.take(pieces[1].reshape(piece_blocks, BLOCK, columns), position, axis=0)]
    dynamic_slice x8 -> x0, local copies, waits for them, and re-layouts: 6.33 us -> none  [shards(): lax.map(row_block, (query_heads.reshape(span_count, row_span, heads, HEAD...]
  transfers between devices with their start and end apart: 2 -> 0, of which waited for: 2 -> 0; matrix products, arithmetic and copies ran while one was open for 2% -> 0% of each run, Pallas kernels for 0% -> 0%
where the time goes in v1:
time: 192 us; the launch traced here: 191 us
  Pallas kernels  185 us (96%)
  local copies, waits for them, and re-layouts  5.61 us (3%)
    pallas_call x1, Pallas kernels, shards(): pl.pallas_call(functools.partial(kernel, views, heads, splits, rows), out...  185 us
    unnamed x14, local copies, waits for them, and re-layouts  5.34 us

profile of v1, /device:TPU:480, one launch (start us, length us, event | category | flops | bytes accessed | tf_op | source)
XLA Modules:
  0.0 191.3 jit_solution(14545737799249132026)
XLA Ops:
  0.0 0.0 copy-start.5
  0.0 0.7 copy-done.5
  0.7 0.1 copy.9
  0.8 0.1 eq.14
  0.9 0.1 fusion
  1.0 0.1 and.23
  1.1 0.4 convert_reduce_fusion
  1.5 0.2 select_reduce_fusion.1
  1.7 0.1 broadcast_add_fusion
  1.8 0.1 add.17
  1.8 0.2 select_reduce_fusion.pos_ref
  2.0 0.0 copy-start.3
  2.0 0.0 copy-start.4
  2.0 0.6 copy-done.3
  2.7 0.0 copy-done.4
  2.7 0.0 copy-start
  2.7 1.0 copy-done
  3.7 0.0 copy-start.1
  3.7 1.0 copy-done.1
  4.8 0.0 copy-start.2
  4.8 1.0 copy-done.2
  5.8 184.6 %shard_map.64 = bf16[2048,128]{1,0:T(8,128)(2,1)S(1)} custom-call(bf16[2048,128]{1,0:T(8,128)(2,1)S(1)} %copy-done, bf16[32,64,128]{2,1,0:T(8,128)(2,1)S(1)} %bitcast.5, bf16[32,64,128]{2,1,0:T(8,128)(2,1)S(1)} %bitcast.6, s32[16,1,128]{2,1,0:T(1,128)S(1)} %bitcast.7, s32[128]{0:T(128)S(1)} %select_reduce_fusion.pos_ref, f32[1,128]{1,0:T(1,128)S(1)} %bitcast.8, ...), custom_call_target="tpu_custom_call" | custom-call | tf_op jit(solution)/shard_map/pallas_call | solution.py:311
  190.5 0.8 copy.11
  (2 shorter events, 0.0 us)
Async XLA Ops:
  0.0 0.7 copy-start.5
  2.0 0.7 copy-start.3
  2.0 0.7 copy-start.4
  2.7 1.0 copy-start
  3.7 1.0 copy-start.1
  4.8 1.0 copy-start.2

commit v2 on v1

--- a/solution.py
+++ b/solution.py
@@ -12,11 +12,10 @@
 TOPK = 4
 CAP = 4
 EPS = 1e-06
-SPLITS = (2, 4, 4)
+SPLITS = (8, 4)
 MESH = pl.DeviceIdType.MESH
 NT = (((1,), (1,)), ((), ()))
 TN = (((0,), (0,)), ((), ()))
-HIGHEST = lax.Precision.HIGHEST
 
 
 def feature(x):
@@ -27,12 +26,12 @@
     return jnp.dot(a, b, preferred_element_type=jnp.float32)
 
 
-def matmul_nt(a, b, precision=None):
-    return lax.dot_general(a, b, NT, precision=precision, preferred_element_type=jnp.float32)
-
-
-def matmul_tn(a, b, precision=None):
-    return lax.dot_general(a, b, TN, precision=precision, preferred_element_type=jnp.float32)
+def matmul_nt(a, b):
+    return lax.dot_general(a, b, NT, preferred_element_type=jnp.float32)
+
+
+def matmul_tn(a, b):
+    return lax.dot_general(a, b, TN, preferred_element_type=jnp.float32)
 
 
 def send_order(views):
@@ -47,16 +46,25 @@
 
 def kernel(
     views, heads, splits, rows,
-    q_ref, k_ref, v_ref, plan_ref, pos_ref, gain_s_ref, gain_l_ref, out_ref,
-    plans, plan_smem, stage, recv, states, entering, leaving, own_state,
+    q_hbm, k_hbm, v_hbm, plan_ref, pos_ref, gain_s_ref, gain_l_ref, out_ref,
+    q_ref, k_ref, v_ref,
+    plans, plan_smem, stage, recv, states, entering, leaving, own_state, members, earlier,
     acc, top, total, att, lin, sums, sums_in,
-    plan_send, plan_recv, bulk_send, bulk_recv, chain_sem, local_sem, sum_send, sum_recv,
+    plan_send, plan_recv, bulk_send, bulk_recv, member_send, member_recv,
+    group_send, group_recv, local_sem, in_sem, sum_send, sum_recv,
 ):
     me = lax.axis_index("view")
     head = lax.axis_index("head")
     scale2 = 1.4426950408889634 * HEAD_DIM ** (-0.5)
     qtile = min(256, rows)
-    qblocks = rows // BLOCK
+    group = 4 if views >= 16 else 2
+
+    k_in = pltpu.make_async_copy(k_hbm, k_ref, in_sem.at[0])
+    v_in = pltpu.make_async_copy(v_hbm, v_ref, in_sem.at[1])
+    q_in = pltpu.make_async_copy(q_hbm, q_ref, in_sem.at[2])
+    k_in.start()
+    v_in.start()
+    q_in.start()
 
     phases = []
     stride = 1
@@ -90,25 +98,52 @@
         def _():
             plan_copy(me, u).start()
 
+    k_in.wait()
+    v_in.wait()
     own_state[...] = matmul_tn(
         feature(k_ref[...].reshape(rows, HEAD_DIM).astype(jnp.float32)).astype(jnp.bfloat16),
         v_ref[...].reshape(rows, HEAD_DIM),
     )
-
-    def chain_copy():
+    leaving[0] = own_state[...].astype(jnp.bfloat16)
+    member = me % group
+
+    def member_copy(slot, step):
         return pltpu.make_async_remote_copy(
-            src_ref=leaving,
-            dst_ref=entering,
-            send_sem=chain_sem.at[0],
-            recv_sem=chain_sem.at[1],
-            device_id=((me + 1) % views, head),
+            src_ref=leaving.at[0],
+            dst_ref=members.at[slot],
+            send_sem=member_send.at[step],
+            recv_sem=member_recv.at[slot],
+            device_id=((me + step) % views, head),
             device_id_type=MESH,
         )
 
-    @pl.when(me == 0)
-    def _():
-        leaving[...] = own_state[...]
-        chain_copy().start()
+    for step in range(1, group):
+        @pl.when(member + step < group)
+        def _():
+            member_copy(member, step).start()
+
+    def group_copy(step):
+        return pltpu.make_async_remote_copy(
+            src_ref=leaving.at[1],
+            dst_ref=earlier,
+            send_sem=group_send.at[step - 1],
+            recv_sem=group_recv,
+            device_id=((me + step) % views, head),
+            device_id_type=MESH,
+        )
+
+    def gather_prefix():
+        entering[...] = jnp.zeros_like(entering)
+        for slot in range(group - 1):
+            @pl.when(slot < member)
+            def _():
+                member_copy(slot, 1).wait_recv()
+                entering[...] += members[slot].astype(jnp.float32)
+
+        @pl.when(me >= group)
+        def _():
+            group_copy(1).wait_recv()
+            entering[...] += earlier[...].astype(jnp.float32)
 
     for w in range(1, views):
         @pl.when(w > me)
@@ -118,6 +153,16 @@
     smem_copy = pltpu.make_async_copy(plans, plan_smem, local_sem)
     smem_copy.start()
     smem_copy.wait()
+
+    @pl.when(member == group - 1)
+    def _():
+        gather_prefix()
+
+        @pl.when(me < views - 1)
+        def _():
+            leaving[1] = (entering[...] + own_state[...]).astype(jnp.bfloat16)
+            for step in range(1, group + 1):
+                group_copy(step).start()
 
     def bulk_copy(slot, to):
         return pltpu.make_async_remote_copy(
@@ -138,15 +183,6 @@
                 stage[w * CAP + s, 1] = v_ref[block]
             bulk_copy(me, w).start()
 
-    @pl.when(me > 0)
-    def _():
-        chain_copy().wait_recv()
-
-        @pl.when(me < views - 1)
-        def _():
-            leaving[...] = entering[...] + own_state[...]
-            chain_copy().start()
-
     row = lax.broadcasted_iota(jnp.int32, (qtile, qtile), 0)
     col = lax.broadcasted_iota(jnp.int32, (qtile, qtile), 1)
 
@@ -154,6 +190,8 @@
 
     def tile_of(ref, j):
         return ref[pl.ds(j * per_tile, per_tile)].reshape(qtile, HEAD_DIM)
+
+    q_in.wait()
 
     @pl.loop(0, rows // qtile)
     def _(i):
@@ -180,6 +218,10 @@
         top[mine, :] = jnp.broadcast_to(m, (qtile, HEAD_DIM))
         total[mine, :] = jnp.broadcast_to(l, (qtile, HEAD_DIM))
 
+    @pl.when(member < group - 1)
+    def _():
+        gather_prefix()
+
     @pl.loop(0, me)
     def _(u):
         bulk_copy(u, u).wait_recv()
@@ -196,45 +238,60 @@
 
     @pl.when(me > 0)
     def _():
-        @pl.loop(0, qblocks)
-        def _(r):
-            mine = pl.ds(pl.multiple_of(r * BLOCK, BLOCK), BLOCK)
+        @pl.loop(0, rows // qtile)
+        def _(i):
+            mine = pl.ds(pl.multiple_of(i * qtile, qtile), qtile)
             q = q_ref[mine, :]
-            scores, values = [], []
-            remaining = entering[...]
-            for c in range(TOPK):
-                at = pos_ref[r * TOPK + c]
-                scores.append(matmul_nt(q, recv[at, 0]))
-                values.append(recv[at, 1])
-                remaining = remaining - states[at]
-            s = jnp.concatenate(scores, axis=1)
+            qf = feature(q.astype(jnp.float32)).astype(jnp.bfloat16)
+            qf = jnp.concatenate([qf, qf], axis=1)
+            scores, values, linear = [], [], []
+            for b in range(per_tile):
+                inside = slice(b * BLOCK, (b + 1) * BLOCK)
+                ats = [pos_ref[(i * per_tile + b) * TOPK + c] for c in range(TOPK)]
+                keys = jnp.concatenate([recv[at, 0] for at in ats], axis=0)
+                scores.append(matmul_nt(q[inside], keys))
+                values.append(jnp.concatenate([recv[at, 1] for at in ats], axis=0))
+                remaining = entering[...]
+                for at in ats:
+                    remaining = remaining - states[at]
+                coarse = remaining.astype(jnp.bfloat16)
+                fine = (remaining - coarse.astype(jnp.float32)).astype(jnp.bfloat16)
+                linear.append(matmul(qf[inside], jnp.concatenate([coarse, fine], axis=0)))
+            lin[mine, :] = jnp.concatenate(linear, axis=0)
+            s = jnp.concatenate(scores, axis=0)
             m_old = top[mine, :][:, :1]
             m = jnp.maximum(m_old, jnp.max(s, axis=1, keepdims=True))
             p = jnp.exp2((s - m) * scale2)
             fade = jnp.exp2((m_old - m) * scale2)
             l = total[mine, :][:, :1] * fade + jnp.sum(p, axis=1, keepdims=True)
-            o = acc[mine, :] * fade + matmul(
-                p.astype(jnp.bfloat16), jnp.concatenate(values, axis=0)
+            p = p.astype(jnp.bfloat16)
+            o = jnp.concatenate(
+                [
+                    matmul(p[b * BLOCK : (b + 1) * BLOCK], values[b])
+                    for b in range(per_tile)
+                ],
+                axis=0,
             )
-            att[mine, :] = o / l
-            qf = feature(q.astype(jnp.float32)).astype(jnp.bfloat16)
-            coarse = remaining.astype(jnp.bfloat16)
-            fine = (remaining - coarse.astype(jnp.float32)).astype(jnp.bfloat16)
-            lin[mine, :] = matmul(qf, coarse) + matmul(qf, fine)
+            att[mine, :] = (acc[mine, :] * fade + o) / l
 
     parts = 4
     seg = rows // parts
-    sub = lax.broadcasted_iota(jnp.int32, (2 * parts, HEAD_DIM), 0)
+    sub = lax.broadcasted_iota(jnp.int32, (2 * parts, 2 * HEAD_DIM), 0)
 
     def pick(i):
-        return jnp.where(sub == i, 1.0, 0.0).astype(jnp.float32)
+        return jnp.where(sub == i, 1.0, 0.0).astype(jnp.bfloat16)
+
+    def halves(x, axis):
+        coarse = x.astype(jnp.bfloat16)
+        fine = (x - coarse.astype(jnp.float32)).astype(jnp.bfloat16)
+        return jnp.concatenate([coarse, fine], axis=axis)
 
     partial = jnp.zeros((2 * parts, seg), jnp.float32)
     for t in range(parts):
         a = att[t * seg : (t + 1) * seg, :]
         b = lin[t * seg : (t + 1) * seg, :]
-        partial = partial + matmul_nt(pick(2 * t), a * a, HIGHEST)
-        partial = partial + matmul_nt(pick(2 * t + 1), b * b, HIGHEST)
+        partial = partial + matmul_nt(pick(2 * t), halves(a * a, 1))
+        partial = partial + matmul_nt(pick(2 * t + 1), halves(b * b, 1))
 
     count = 0
     copies = []
@@ -260,10 +317,14 @@
 
     scales = lax.rsqrt(partial / (heads * HEAD_DIM) + EPS)
     gain_s, gain_l = gain_s_ref[...], gain_l_ref[...]
+    spread = halves(scales, 0)
+    lane = lax.broadcasted_iota(jnp.int32, (4 * parts, 2 * HEAD_DIM), 1)
+    which = lax.broadcasted_iota(jnp.int32, (4 * parts, 2 * HEAD_DIM), 0) % (2 * parts)
     for t in range(parts):
         span = slice(t * seg, (t + 1) * seg)
-        soft = matmul_tn(scales, pick(2 * t), HIGHEST)
-        linear = matmul_tn(scales, pick(2 * t + 1), HIGHEST)
+        target = jnp.where(lane < HEAD_DIM, 2 * t, 2 * t + 1)
+        both = matmul_tn(spread, jnp.where(which == target, 1.0, 0.0).astype(jnp.bfloat16))
+        soft, linear = both[:, :HEAD_DIM], both[:, HEAD_DIM:]
         out_ref[span, :] = (
             att[span, :] * soft * gain_s + lin[span, :] * linear * gain_l
         ).astype(jnp.bfloat16)
@@ -279,9 +340,15 @@
         def _():
             bulk_copy(me, w).wait_send()
 
-    @pl.when(me < views - 1)
+    for step in range(1, group):
+        @pl.when(member + step < group)
+        def _():
+            member_copy(member, step).wait_send()
+
+    @pl.when((member == group - 1) & (me < views - 1))
     def _():
-        chain_copy().wait_send()
+        for step in range(1, group + 1):
+            group_copy(step).wait_send()
 
 
 def shards(views, heads, splits, q, k, v, lists, gain_s, gain_l):
@@ -305,23 +372,29 @@
     partners = sum(s - 1 for s in splits)
     f32, bf16 = jnp.float32, jnp.bfloat16
     vmem = pl.BlockSpec(memory_space=pltpu.VMEM)
+    hbm = pl.BlockSpec(memory_space=pl.ANY)
     smem = pl.BlockSpec(memory_space=pltpu.SMEM)
     dma = pltpu.SemaphoreType.DMA
     sums = (8, rows // 4)
     return pl.pallas_call(
         functools.partial(kernel, views, heads, splits, rows),
         out_shape=jax.ShapeDtypeStruct(q.shape, bf16),
-        in_specs=[vmem, vmem, vmem, vmem, smem, vmem, vmem],
+        in_specs=[hbm, hbm, hbm, vmem, smem, vmem, vmem],
         out_specs=vmem,
         scratch_shapes=[
+            pltpu.VMEM((rows, HEAD_DIM), bf16),
+            pltpu.VMEM((per_view, BLOCK, HEAD_DIM), bf16),
+            pltpu.VMEM((per_view, BLOCK, HEAD_DIM), bf16),
             pltpu.VMEM((views, 1, HEAD_DIM), jnp.int32),
             pltpu.SMEM((views, 1, HEAD_DIM), jnp.int32),
             pltpu.VMEM((views * CAP, 2, BLOCK, HEAD_DIM), bf16),
             pltpu.VMEM((views * CAP, 2, BLOCK, HEAD_DIM), bf16),
             pltpu.VMEM((views * CAP, HEAD_DIM, HEAD_DIM), f32),
             pltpu.VMEM((HEAD_DIM, HEAD_DIM), f32),
+            pltpu.VMEM((2, HEAD_DIM, HEAD_DIM), bf16),
             pltpu.VMEM((HEAD_DIM, HEAD_DIM), f32),
-            pltpu.VMEM((HEAD_DIM, HEAD_DIM), f32),
+            pltpu.VMEM((3, HEAD_DIM, HEAD_DIM), bf16),
+            pltpu.VMEM((HEAD_DIM, HEAD_DIM), bf16),
             pltpu.VMEM((rows, HEAD_DIM), f32),
             pltpu.VMEM((rows, HEAD_DIM), f32),
             pltpu.VMEM((rows, HEAD_DIM), f32),
@@ -333,8 +406,12 @@
             dma((views,)),
             dma((views,)),
             dma((views,)),
-            dma((2,)),
+            dma((4,)),
+            dma((4,)),
+            dma((4,)),
             dma,
+            dma,
+            dma((3,)),
             dma((partners,)),
             dma((partners,)),
         ],

time: 192 us -> 139 us (0.72)
  the two profiles are of different devices: /device:TPU:480 before, /device:TPU:384 now
where the time goes in v2:
time: 139 us
  Pallas kernels  132 us (95%)
  local copies, waits for them, and re-layouts  5.61 us (4%)
    pallas_call x1, Pallas kernels, shards(): pl.pallas_call(functools.partial(kernel, views, heads, splits, rows), out...  132 us
    unnamed x14, local copies, waits for them, and re-layouts  5.34 us

profile of v2, /device:TPU:384, one launch (start us, length us, event | category | flops | bytes accessed | tf_op | source)
XLA Modules:
  0.0 138.9 jit_solution(2421824884846798572)
XLA Ops:
  0.0 0.0 copy-start.5
  0.0 0.7 copy-done.5
  0.7 0.1 copy.9
  0.8 0.1 eq.14
  0.9 0.1 fusion
  1.0 0.1 and.23
  1.1 0.4 convert_reduce_fusion
  1.5 0.2 select_reduce_fusion.1
  1.7 0.1 broadcast_add_fusion
  1.8 0.1 add.17
  1.8 0.2 select_reduce_fusion.pos_ref
  2.0 0.0 copy-start.3
  2.0 0.0 copy-start.4
  2.0 0.6 copy-done.3
  2.7 0.0 copy-done.4
  2.7 0.0 copy-start
  2.7 1.0 copy-done
  3.7 0.0 copy-start.1
  3.7 1.0 copy-done.1
  4.8 0.0 copy-start.2
  4.8 1.0 copy-done.2
  5.8 132.3 %shard_map.64 = bf16[2048,128]{1,0:T(8,128)(2,1)S(1)} custom-call(bf16[2048,128]{1,0:T(8,128)(2,1)S(1)} %copy-done, bf16[32,64,128]{2,1,0:T(8,128)(2,1)S(1)} %bitcast.5, bf16[32,64,128]{2,1,0:T(8,128)(2,1)S(1)} %bitcast.6, s32[16,1,128]{2,1,0:T(1,128)S(1)} %bitcast.7, s32[128]{0:T(128)S(1)} %select_reduce_fusion.pos_ref, f32[1,128]{1,0:T(1,128)S(1)} %bitcast.8, ...), custom_call_target="tpu_custom_call" | custom-call | tf_op jit(solution)/shard_map/pallas_call | solution.py:379
  138.1 0.8 copy.11
  (2 shorter events, 0.0 us)
Async XLA Ops:
  0.0 0.7 copy-start.5
  2.0 0.7 copy-start.3
  2.0 0.7 copy-start.4
  2.7 1.0 copy-start
  3.7 1.0 copy-start.1
  4.8 1.0 copy-start.2

commit v3 on v2

--- a/solution.py
+++ b/solution.py
@@ -34,6 +34,12 @@
     return lax.dot_general(a, b, TN, preferred_element_type=jnp.float32)
 
 
+def halves(x, axis):
+    coarse = x.astype(jnp.bfloat16)
+    fine = (x - coarse.astype(jnp.float32)).astype(jnp.bfloat16)
+    return jnp.concatenate([coarse, fine], axis=axis)
+
+
 def send_order(views):
     half = views // 2
     low, high = list(range(half, views)), []
@@ -44,11 +50,36 @@
     return high + list(range(half - 1, 0, -1))
 
 
+def listing(views, per_view, lists_ref, plan_ref, place_ref):
+    blocks = views * per_view
+    ids = lax.broadcasted_iota(jnp.int32, (blocks, per_view), 0)
+    ones = [jnp.where(lists_ref[c : c + 1, :] == ids, 1.0, 0.0) for c in range(TOPK)]
+    count = matmul(
+        sum(ones).astype(jnp.bfloat16), jnp.ones((per_view, HEAD_DIM), jnp.bfloat16)
+    )
+    present = jnp.where(count > 0.0, 1.0, 0.0)
+    down = lax.broadcasted_iota(jnp.int32, (blocks, blocks), 0)
+    across = lax.broadcasted_iota(jnp.int32, (blocks, blocks), 1)
+    before = (across < down) & (across >= down - down % per_view)
+    rank = matmul(jnp.where(before, 1.0, 0.0).astype(jnp.bfloat16), present.astype(jnp.bfloat16))
+    ident = lax.broadcasted_iota(jnp.int32, (blocks, HEAD_DIM), 0)
+    slot = lax.broadcasted_iota(jnp.int32, (blocks, HEAD_DIM), 1).astype(jnp.float32)
+    number = jnp.where(rank == slot, present * (ident % per_view).astype(jnp.float32), 0.0)
+    for u in range(views):
+        plan_ref[u] = jnp.sum(
+            number[u * per_view : (u + 1) * per_view], axis=0, keepdims=True
+        ).astype(jnp.int32)
+    place = ((ident // per_view * CAP).astype(jnp.float32) + rank)[:, :per_view]
+    place_ref[...] = jnp.zeros_like(place_ref)
+    for c in range(TOPK):
+        place_ref[c : c + 1, :per_view] = jnp.sum(ones[c] * place, axis=0, keepdims=True).astype(jnp.int32)
+
+
 def kernel(
     views, heads, splits, rows,
-    q_hbm, k_hbm, v_hbm, plan_ref, pos_ref, gain_s_ref, gain_l_ref, out_ref,
-    q_ref, k_ref, v_ref,
-    plans, plan_smem, stage, recv, states, entering, leaving, own_state, members, earlier,
+    q_hbm, k_hbm, v_hbm, plan_hbm, place_hbm, gain_s_hbm, gain_l_hbm, out_ref,
+    q_ref, k_ref, v_ref, gains,
+    plan_ref, pos_ref, plans, plan_smem, stage, recv, states, entering, leaving, own_state, members, earlier,
     acc, top, total, att, lin, sums, sums_in,
     plan_send, plan_recv, bulk_send, bulk_recv, member_send, member_recv,
     group_send, group_recv, local_sem, in_sem, sum_send, sum_recv,
@@ -65,6 +96,12 @@
     k_in.start()
     v_in.start()
     q_in.start()
+    gain_in = [
+        pltpu.make_async_copy(gain_s_hbm, gains.at[0], in_sem.at[3]),
+        pltpu.make_async_copy(gain_l_hbm, gains.at[1], in_sem.at[4]),
+    ]
+    for copy in gain_in:
+        copy.start()
 
     phases = []
     stride = 1
@@ -72,6 +109,11 @@
         place = head // stride % size
         phases.append([head + ((place + t) % size - place) * stride for t in range(1, size)])
         stride *= size
+
+    plan_in = pltpu.make_async_copy(plan_hbm, plan_ref, local_sem)
+    plan_in.start()
+    place_in = pltpu.make_async_copy(place_hbm, pos_ref, in_sem.at[5])
+    place_in.start()
 
     barrier = pltpu.get_barrier_semaphore()
     for d in range(1, views):
@@ -83,6 +125,8 @@
             pl.semaphore_signal(barrier, inc=1, device_id=(me, other), device_id_type=MESH)
     pl.semaphore_wait(barrier, views - 1 + sum(len(p) for p in phases))
 
+    plan_in.wait()
+
     def plan_copy(slot, to):
         return pltpu.make_async_remote_copy(
             src_ref=plan_ref.at[to],
@@ -150,9 +194,10 @@
         def _():
             plan_copy(w, w).wait_recv()
 
-    smem_copy = pltpu.make_async_copy(plans, plan_smem, local_sem)
-    smem_copy.start()
-    smem_copy.wait()
+
+    plans_copy = pltpu.make_async_copy(plans, plan_smem, local_sem)
+    plans_copy.start()
+    plans_copy.wait()
 
     @pl.when(member == group - 1)
     def _():
@@ -192,6 +237,9 @@
         return ref[pl.ds(j * per_tile, per_tile)].reshape(qtile, HEAD_DIM)
 
     q_in.wait()
+    place_in.wait()
+    for copy in gain_in:
+        copy.wait()
 
     @pl.loop(0, rows // qtile)
     def _(i):
@@ -236,100 +284,111 @@
         att[...] = acc[...] / total[...]
         lin[...] = jnp.zeros_like(lin)
 
-    @pl.when(me > 0)
-    def _():
-        @pl.loop(0, rows // qtile)
-        def _(i):
-            mine = pl.ds(pl.multiple_of(i * qtile, qtile), qtile)
-            q = q_ref[mine, :]
-            qf = feature(q.astype(jnp.float32)).astype(jnp.bfloat16)
-            qf = jnp.concatenate([qf, qf], axis=1)
-            scores, values, linear = [], [], []
-            for b in range(per_tile):
-                inside = slice(b * BLOCK, (b + 1) * BLOCK)
-                ats = [pos_ref[(i * per_tile + b) * TOPK + c] for c in range(TOPK)]
-                keys = jnp.concatenate([recv[at, 0] for at in ats], axis=0)
-                scores.append(matmul_nt(q[inside], keys))
-                values.append(jnp.concatenate([recv[at, 1] for at in ats], axis=0))
-                remaining = entering[...]
-                for at in ats:
-                    remaining = remaining - states[at]
-                coarse = remaining.astype(jnp.bfloat16)
-                fine = (remaining - coarse.astype(jnp.float32)).astype(jnp.bfloat16)
-                linear.append(matmul(qf[inside], jnp.concatenate([coarse, fine], axis=0)))
-            lin[mine, :] = jnp.concatenate(linear, axis=0)
-            s = jnp.concatenate(scores, axis=0)
-            m_old = top[mine, :][:, :1]
-            m = jnp.maximum(m_old, jnp.max(s, axis=1, keepdims=True))
-            p = jnp.exp2((s - m) * scale2)
-            fade = jnp.exp2((m_old - m) * scale2)
-            l = total[mine, :][:, :1] * fade + jnp.sum(p, axis=1, keepdims=True)
-            p = p.astype(jnp.bfloat16)
-            o = jnp.concatenate(
-                [
-                    matmul(p[b * BLOCK : (b + 1) * BLOCK], values[b])
-                    for b in range(per_tile)
-                ],
-                axis=0,
-            )
-            att[mine, :] = (acc[mine, :] * fade + o) / l
+    def listed(start):
+        mine = slice(start, start + qtile)
+        q = q_ref[mine, :]
+        qf = feature(q.astype(jnp.float32)).astype(jnp.bfloat16)
+        qf = jnp.concatenate([qf, qf], axis=1)
+        scores, values, linear = [], [], []
+        for b in range(per_tile):
+            inside = slice(b * BLOCK, (b + 1) * BLOCK)
+            ats = [pos_ref[c, start // BLOCK + b] for c in range(TOPK)]
+            keys = jnp.concatenate([recv[at, 0] for at in ats], axis=0)
+            scores.append(matmul_nt(q[inside], keys))
+            values.append(jnp.concatenate([recv[at, 1] for at in ats], axis=0))
+            remaining = entering[...]
+            for at in ats:
+                remaining = remaining - states[at]
+            linear.append(matmul(qf[inside], halves(remaining, 0)))
+        s = jnp.concatenate(scores, axis=0)
+        m_old = top[mine, :][:, :1]
+        m = jnp.maximum(m_old, jnp.max(s, axis=1, keepdims=True))
+        p = jnp.exp2((s - m) * scale2)
+        fade = jnp.exp2((m_old - m) * scale2)
+        l = total[mine, :][:, :1] * fade + jnp.sum(p, axis=1, keepdims=True)
+        p = p.astype(jnp.bfloat16)
+        o = jnp.concatenate(
+            [matmul(p[b * BLOCK : (b + 1) * BLOCK], values[b]) for b in range(per_tile)],
+            axis=0,
+        )
+        return (acc[mine, :] * fade + o) / l, jnp.concatenate(linear, axis=0)
 
     parts = 4
     seg = rows // parts
-    sub = lax.broadcasted_iota(jnp.int32, (2 * parts, 2 * HEAD_DIM), 0)
+    chunk = min(seg, HEAD_DIM)
+    chunks = seg // chunk
+    height = 2 * chunks
+    sub = lax.broadcasted_iota(jnp.int32, (height, 2 * HEAD_DIM), 0)
 
     def pick(i):
         return jnp.where(sub == i, 1.0, 0.0).astype(jnp.bfloat16)
 
-    def halves(x, axis):
-        coarse = x.astype(jnp.bfloat16)
-        fine = (x - coarse.astype(jnp.float32)).astype(jnp.bfloat16)
-        return jnp.concatenate([coarse, fine], axis=axis)
-
-    partial = jnp.zeros((2 * parts, seg), jnp.float32)
-    for t in range(parts):
-        a = att[t * seg : (t + 1) * seg, :]
-        b = lin[t * seg : (t + 1) * seg, :]
-        partial = partial + matmul_nt(pick(2 * t), halves(a * a, 1))
-        partial = partial + matmul_nt(pick(2 * t + 1), halves(b * b, 1))
-
-    count = 0
-    copies = []
-    for phase, partners in enumerate(phases):
-        sums[phase] = partial
-        here = []
-        for other in partners:
+    def squares(t):
+        partial = jnp.zeros((height, chunk), jnp.float32)
+        for c in range(chunks):
+            span = slice(t * seg + c * chunk, t * seg + (c + 1) * chunk)
+            a, b = att[span, :], lin[span, :]
+            partial = partial + matmul_nt(pick(2 * c), halves(a * a, 1))
+            partial = partial + matmul_nt(pick(2 * c + 1), halves(b * b, 1))
+        return partial
+
+    sent = []
+    waiting = {}
+
+    def exchange(t, phase, partial):
+        sums[t, phase] = partial
+        base = sum(len(p) for p in phases[:phase])
+        waiting[t, phase] = []
+        for n, other in enumerate(phases[phase]):
             copy = pltpu.make_async_remote_copy(
-                src_ref=sums.at[phase],
-                dst_ref=sums_in.at[count],
-                send_sem=sum_send.at[count],
-                recv_sem=sum_recv.at[count],
+                src_ref=sums.at[t, phase],
+                dst_ref=sums_in.at[t, base + n],
+                send_sem=sum_send.at[t, base + n],
+                recv_sem=sum_recv.at[t, base + n],
                 device_id=(me, other),
                 device_id_type=MESH,
             )
             copy.start()
-            here.append((copy, count))
-            count += 1
-        for copy, at in here:
+            waiting[t, phase].append((copy, base + n))
+            sent.append(copy)
+
+    def collect(t, phase):
+        partial = sums[t, phase]
+        for copy, at in waiting[t, phase]:
             copy.wait_recv()
-            partial = partial + sums_in[at]
-        copies += [copy for copy, _ in here]
-
-    scales = lax.rsqrt(partial / (heads * HEAD_DIM) + EPS)
-    gain_s, gain_l = gain_s_ref[...], gain_l_ref[...]
-    spread = halves(scales, 0)
-    lane = lax.broadcasted_iota(jnp.int32, (4 * parts, 2 * HEAD_DIM), 1)
-    which = lax.broadcasted_iota(jnp.int32, (4 * parts, 2 * HEAD_DIM), 0) % (2 * parts)
+            partial = partial + sums_in[t, at]
+        return partial
+
+    def finish(t):
+        spread = halves(lax.rsqrt(collect(t, 1) / (heads * HEAD_DIM) + EPS), 0)
+        lane = lax.broadcasted_iota(jnp.int32, (2 * height, 2 * HEAD_DIM), 1)
+        which = lax.broadcasted_iota(jnp.int32, (2 * height, 2 * HEAD_DIM), 0) % height
+        for c in range(chunks):
+            span = slice(t * seg + c * chunk, t * seg + (c + 1) * chunk)
+            target = jnp.where(lane < HEAD_DIM, 2 * c, 2 * c + 1)
+            both = matmul_tn(spread, jnp.where(which == target, 1.0, 0.0).astype(jnp.bfloat16))
+            out_ref[span, :] = (
+                att[span, :] * both[:, :HEAD_DIM] * gains[0]
+                + lin[span, :] * both[:, HEAD_DIM:] * gains[1]
+            ).astype(jnp.bfloat16)
+
     for t in range(parts):
-        span = slice(t * seg, (t + 1) * seg)
-        target = jnp.where(lane < HEAD_DIM, 2 * t, 2 * t + 1)
-        both = matmul_tn(spread, jnp.where(which == target, 1.0, 0.0).astype(jnp.bfloat16))
-        soft, linear = both[:, :HEAD_DIM], both[:, HEAD_DIM:]
-        out_ref[span, :] = (
-            att[span, :] * soft * gain_s + lin[span, :] * linear * gain_l
-        ).astype(jnp.bfloat16)
-
-    for copy in copies:
+        @pl.when(me > 0)
+        def _():
+            for start in range(t * seg, (t + 1) * seg, qtile):
+                attended, linear = listed(start)
+                att[start : start + qtile, :] = attended
+                lin[start : start + qtile, :] = linear
+
+        exchange(t, 0, squares(t))
+        if t > 0:
+            exchange(t - 1, 1, collect(t - 1, 0))
+    finish(0)
+    exchange(parts - 1, 1, collect(parts - 1, 0))
+    for t in range(1, parts):
+        finish(t)
+
+    for copy in sent:
         copy.wait_send()
     for u in range(views - 1):
         @pl.when(u < me)
@@ -354,37 +413,37 @@
 def shards(views, heads, splits, q, k, v, lists, gain_s, gain_l):
     rows = q.shape[0]
     per_view = rows // BLOCK
-    blocks = views * per_view
-    flat = lists.reshape(-1)
-    ids = jnp.arange(blocks, dtype=jnp.int32)
-    present = jnp.any(flat[:, None] == ids[None, :], axis=0)
-    table = present.reshape(views, per_view)
-    within = jnp.arange(per_view, dtype=jnp.int32)
-    earlier = within[None, :] < within[:, None]
-    rank = jnp.sum(table[:, None, :] & earlier[None], axis=2, dtype=jnp.int32)
-    slots = jnp.arange(HEAD_DIM, dtype=jnp.int32)
-    chosen = table[:, None, :] & (rank[:, None, :] == slots[None, :, None])
-    plan = jnp.sum(jnp.where(chosen, within[None, None, :], 0), axis=2, dtype=jnp.int32)
-    place = (jnp.arange(views, dtype=jnp.int32)[:, None] * CAP + rank).reshape(-1)
-    pos = jnp.sum(jnp.where(flat[:, None] == ids[None, :], place[None, :], 0), axis=1)
+    plan, place = pl.pallas_call(
+        functools.partial(listing, views, per_view),
+        out_shape=(
+            jax.ShapeDtypeStruct((views, 1, HEAD_DIM), jnp.int32),
+            jax.ShapeDtypeStruct((TOPK, HEAD_DIM), jnp.int32),
+        ),
+        in_specs=[pl.BlockSpec(memory_space=pltpu.VMEM)],
+        out_specs=(pl.BlockSpec(memory_space=pltpu.VMEM),) * 2,
+    )(lists.T)
 
     phases = len(splits)
     partners = sum(s - 1 for s in splits)
     f32, bf16 = jnp.float32, jnp.bfloat16
     vmem = pl.BlockSpec(memory_space=pltpu.VMEM)
-    hbm = pl.BlockSpec(memory_space=pl.ANY)
-    smem = pl.BlockSpec(memory_space=pltpu.SMEM)
+    hbm = pl.BlockSpec(memory_space=pltpu.HBM)
     dma = pltpu.SemaphoreType.DMA
-    sums = (8, rows // 4)
+    parts = 4
+    chunk = min(rows // parts, HEAD_DIM)
+    sums = (2 * (rows // parts // chunk), chunk)
     return pl.pallas_call(
         functools.partial(kernel, views, heads, splits, rows),
         out_shape=jax.ShapeDtypeStruct(q.shape, bf16),
-        in_specs=[hbm, hbm, hbm, vmem, smem, vmem, vmem],
+        in_specs=[hbm] * 7,
         out_specs=vmem,
         scratch_shapes=[
             pltpu.VMEM((rows, HEAD_DIM), bf16),
             pltpu.VMEM((per_view, BLOCK, HEAD_DIM), bf16),
             pltpu.VMEM((per_view, BLOCK, HEAD_DIM), bf16),
+            pltpu.VMEM((2, 1, HEAD_DIM), f32),
+            pltpu.VMEM((views, 1, HEAD_DIM), jnp.int32),
+            pltpu.SMEM((TOPK, HEAD_DIM), jnp.int32),
             pltpu.VMEM((views, 1, HEAD_DIM), jnp.int32),
             pltpu.SMEM((views, 1, HEAD_DIM), jnp.int32),
             pltpu.VMEM((views * CAP, 2, BLOCK, HEAD_DIM), bf16),
@@ -400,8 +459,8 @@
             pltpu.VMEM((rows, HEAD_DIM), f32),
             pltpu.VMEM((rows, HEAD_DIM), f32),
             pltpu.VMEM((rows, HEAD_DIM), f32),
-            pltpu.VMEM((phases,) + sums, f32),
-            pltpu.VMEM((partners,) + sums, f32),
+            pltpu.VMEM((parts, phases) + sums, f32),
+            pltpu.VMEM((parts, partners) + sums, f32),
             dma((views,)),
             dma((views,)),
             dma((views,)),
@@ -411,19 +470,19 @@
             dma((4,)),
             dma,
             dma,
-            dma((3,)),
-            dma((partners,)),
-            dma((partners,)),
+            dma((6,)),
+            dma((parts, partners)),
+            dma((parts, partners)),
         ],
         compiler_params=pltpu.CompilerParams(
-            collective_id=0, has_side_effects=True, vmem_limit_bytes=48 * 1024 * 1024
+            collective_id=0, has_side_effects=True, vmem_limit_bytes=56 * 1024 * 1024
         ),
     )(
         q,
         k.reshape(per_view, BLOCK, HEAD_DIM),
         v.reshape(per_view, BLOCK, HEAD_DIM),
-        plan.reshape(views, 1, HEAD_DIM),
-        pos,
+        plan,
+        place,
         gain_s[None],
         gain_l[None],
     )

time: 139 us -> 136 us (0.978)
  local copies, waits for them, and re-layouts: 5.61 us -> 1.87 us
  Pallas kernels: 132 us -> 134 us
    unnamed x14 -> x1, local copies, waits for them, and re-layouts: 5.34 us -> 1.87 us
    pallas_call x0 -> x1, Pallas kernels: none -> 1.83 us  [shards(): pl.pallas_call(functools.partial(listing, views, per_view), out_shape=(ja...]
where the time goes in v3:
time: 136 us
  Pallas kernels  134 us (99%)
  local copies, waits for them, and re-layouts  1.87 us (1%)
    pallas_call x1, Pallas kernels, shards(): pl.pallas_call(functools.partial(kernel, views, heads, splits, rows), out...  132 us

profile of v3, /device:TPU:384, one launch (start us, length us, event | category | flops | bytes accessed | tf_op | source)
XLA Modules:
  0.0 136.2 jit_solution(17744631627707797595)
XLA Ops:
  0.0 1.8 %shard_map.64 = (s32[16,1,128]{2,1,0:T(1,128)}, s32[4,128]{1,0:T(4,128)}) custom-call(s32[4,32]{1,0:T(4,128)} %bitcast.7), custom_call_target="tpu_custom_call" | custom-call | tf_op jit(solution)/shard_map/pallas_call | solution.py:416
  1.8 132.5 %shard_map.65 = bf16[2048,128]{1,0:T(8,128)(2,1)} custom-call(bf16[2048,128]{1,0:T(8,128)(2,1)} %q_hbm.1, bf16[32,64,128]{2,1,0:T(8,128)(2,1)} %bitcast.5, bf16[32,64,128]{2,1,0:T(8,128)(2,1)} %bitcast.6, s32[16,1,128]{2,1,0:T(1,128)} %get-tuple-element.7.plan_hbm, s32[4,128]{1,0:T(4,128)} %get-tuple-element.8.place_hbm, f32[1,128]{1,0:T(1,128)} %bitcast.8, ...), custom_call_target="tpu_custom_call" | custom-call | tf_op jit(solution)/shard_map/pallas_call | solution.py:435
  134.3 1.9 %copy.8 = bf16[2048,128]{1,0:T(8,128)(2,1)} copy(bf16[2048,128]{1,0:T(8,128)(2,1)} %shard_map.65) | data formatting | bytes 1048576

commit v4 on v3

--- a/solution.py
+++ b/solution.py
@@ -50,7 +50,54 @@
     return high + list(range(half - 1, 0, -1))
 
 
-def listing(views, per_view, lists_ref, plan_ref, place_ref):
+def kernel(
+    views, heads, splits, rows,
+    q_hbm, k_hbm, v_hbm, lists_hbm, gain_s_hbm, gain_l_hbm, out_ref,
+    q_ref, k_ref, v_ref, gains,
+    lists_ref, plan_ref, place_ref, pos_ref, plans, plan_smem, stage, recv, states, entering, leaving, own_state, members, earlier,
+    acc, top, total, att, lin, sums, sums_in,
+    plan_send, plan_recv, bulk_send, bulk_recv, member_send, member_recv,
+    group_send, group_recv, local_sem, in_sem, sum_send, sum_recv,
+):
+    me = lax.axis_index("view")
+    head = lax.axis_index("head")
+    scale2 = 1.4426950408889634 * HEAD_DIM ** (-0.5)
+    qtile = min(256, rows)
+    group = 4 if views >= 16 else 2
+
+    k_in = pltpu.make_async_copy(k_hbm, k_ref, in_sem.at[0])
+    v_in = pltpu.make_async_copy(v_hbm, v_ref, in_sem.at[1])
+    q_in = pltpu.make_async_copy(q_hbm, q_ref, in_sem.at[2])
+    k_in.start()
+    v_in.start()
+    q_in.start()
+    gain_in = [
+        pltpu.make_async_copy(gain_s_hbm, gains.at[0], in_sem.at[3]),
+        pltpu.make_async_copy(gain_l_hbm, gains.at[1], in_sem.at[4]),
+    ]
+    for copy in gain_in:
+        copy.start()
+
+    phases = []
+    stride = 1
+    for size in splits:
+        place = head // stride % size
+        phases.append([head + ((place + t) % size - place) * stride for t in range(1, size)])
+        stride *= size
+
+    lists_in = pltpu.make_async_copy(lists_hbm, lists_ref, local_sem)
+    lists_in.start()
+
+    barrier = pltpu.get_barrier_semaphore()
+    for d in range(1, views):
+        pl.semaphore_signal(
+            barrier, inc=1, device_id=((me + d) % views, head), device_id_type=MESH
+        )
+    for partners in phases:
+        for other in partners:
+            pl.semaphore_signal(barrier, inc=1, device_id=(me, other), device_id_type=MESH)
+    lists_in.wait()
+    per_view = rows // BLOCK
     blocks = views * per_view
     ids = lax.broadcasted_iota(jnp.int32, (blocks, per_view), 0)
     ones = [jnp.where(lists_ref[c : c + 1, :] == ids, 1.0, 0.0) for c in range(TOPK)]
@@ -66,66 +113,17 @@
     slot = lax.broadcasted_iota(jnp.int32, (blocks, HEAD_DIM), 1).astype(jnp.float32)
     number = jnp.where(rank == slot, present * (ident % per_view).astype(jnp.float32), 0.0)
     for u in range(views):
-        plan_ref[u] = jnp.sum(
-            number[u * per_view : (u + 1) * per_view], axis=0, keepdims=True
-        ).astype(jnp.int32)
+        listed_here = jnp.sum(number[u * per_view : (u + 1) * per_view], axis=0, keepdims=True)
+        plan_ref[u] = jnp.clip(listed_here.astype(jnp.int32), 0, per_view - 1)
     place = ((ident // per_view * CAP).astype(jnp.float32) + rank)[:, :per_view]
     place_ref[...] = jnp.zeros_like(place_ref)
     for c in range(TOPK):
-        place_ref[c : c + 1, :per_view] = jnp.sum(ones[c] * place, axis=0, keepdims=True).astype(jnp.int32)
-
-
-def kernel(
-    views, heads, splits, rows,
-    q_hbm, k_hbm, v_hbm, plan_hbm, place_hbm, gain_s_hbm, gain_l_hbm, out_ref,
-    q_ref, k_ref, v_ref, gains,
-    plan_ref, pos_ref, plans, plan_smem, stage, recv, states, entering, leaving, own_state, members, earlier,
-    acc, top, total, att, lin, sums, sums_in,
-    plan_send, plan_recv, bulk_send, bulk_recv, member_send, member_recv,
-    group_send, group_recv, local_sem, in_sem, sum_send, sum_recv,
-):
-    me = lax.axis_index("view")
-    head = lax.axis_index("head")
-    scale2 = 1.4426950408889634 * HEAD_DIM ** (-0.5)
-    qtile = min(256, rows)
-    group = 4 if views >= 16 else 2
-
-    k_in = pltpu.make_async_copy(k_hbm, k_ref, in_sem.at[0])
-    v_in = pltpu.make_async_copy(v_hbm, v_ref, in_sem.at[1])
-    q_in = pltpu.make_async_copy(q_hbm, q_ref, in_sem.at[2])
-    k_in.start()
-    v_in.start()
-    q_in.start()
-    gain_in = [
-        pltpu.make_async_copy(gain_s_hbm, gains.at[0], in_sem.at[3]),
-        pltpu.make_async_copy(gain_l_hbm, gains.at[1], in_sem.at[4]),
-    ]
-    for copy in gain_in:
-        copy.start()
-
-    phases = []
-    stride = 1
-    for size in splits:
-        place = head // stride % size
-        phases.append([head + ((place + t) % size - place) * stride for t in range(1, size)])
-        stride *= size
-
-    plan_in = pltpu.make_async_copy(plan_hbm, plan_ref, local_sem)
-    plan_in.start()
-    place_in = pltpu.make_async_copy(place_hbm, pos_ref, in_sem.at[5])
+        entry = jnp.sum(ones[c] * place, axis=0, keepdims=True).astype(jnp.int32)
+        place_ref[c : c + 1, :per_view] = jnp.clip(entry, 0, views * CAP - 1)
+    place_in = pltpu.make_async_copy(place_ref, pos_ref, in_sem.at[5])
     place_in.start()
 
-    barrier = pltpu.get_barrier_semaphore()
-    for d in range(1, views):
-        pl.semaphore_signal(
-            barrier, inc=1, device_id=((me + d) % views, head), device_id_type=MESH
-        )
-    for partners in phases:
-        for other in partners:
-            pl.semaphore_signal(barrier, inc=1, device_id=(me, other), device_id_type=MESH)
     pl.semaphore_wait(barrier, views - 1 + sum(len(p) for p in phases))
-
-    plan_in.wait()
 
     def plan_copy(slot, to):
         return pltpu.make_async_remote_copy(
@@ -166,9 +164,9 @@
         def _():
             member_copy(member, step).start()
 
-    def group_copy(step):
+    def group_copy(step, source):
         return pltpu.make_async_remote_copy(
-            src_ref=leaving.at[1],
+            src_ref=source,
             dst_ref=earlier,
             send_sem=group_send.at[step - 1],
             recv_sem=group_recv,
@@ -186,8 +184,13 @@
 
         @pl.when(me >= group)
         def _():
-            group_copy(1).wait_recv()
+            group_copy(1, earlier).wait_recv()
             entering[...] += earlier[...].astype(jnp.float32)
+
+            @pl.when(member == 0)
+            def _():
+                for step in range(1, group - 1):
+                    group_copy(step, earlier).start()
 
     for w in range(1, views):
         @pl.when(w > me)
@@ -206,8 +209,8 @@
         @pl.when(me < views - 1)
         def _():
             leaving[1] = (entering[...] + own_state[...]).astype(jnp.bfloat16)
-            for step in range(1, group + 1):
-                group_copy(step).start()
+            for step in (1, group):
+                group_copy(step, leaving.at[1]).start()
 
     def bulk_copy(slot, to):
         return pltpu.make_async_remote_copy(
@@ -406,23 +409,18 @@
 
     @pl.when((member == group - 1) & (me < views - 1))
     def _():
-        for step in range(1, group + 1):
-            group_copy(step).wait_send()
+        for step in (1, group):
+            group_copy(step, leaving.at[1]).wait_send()
+
+    @pl.when((member == 0) & (me >= group))
+    def _():
+        for step in range(1, group - 1):
+            group_copy(step, earlier).wait_send()
 
 
 def shards(views, heads, splits, q, k, v, lists, gain_s, gain_l):
     rows = q.shape[0]
     per_view = rows // BLOCK
-    plan, place = pl.pallas_call(
-        functools.partial(listing, views, per_view),
-        out_shape=(
-            jax.ShapeDtypeStruct((views, 1, HEAD_DIM), jnp.int32),
-            jax.ShapeDtypeStruct((TOPK, HEAD_DIM), jnp.int32),
-        ),
-        in_specs=[pl.BlockSpec(memory_space=pltpu.VMEM)],
-        out_specs=(pl.BlockSpec(memory_space=pltpu.VMEM),) * 2,
-    )(lists.T)
-
     phases = len(splits)
     partners = sum(s - 1 for s in splits)
     f32, bf16 = jnp.float32, jnp.bfloat16
@@ -435,14 +433,16 @@
     return pl.pallas_call(
         functools.partial(kernel, views, heads, splits, rows),
         out_shape=jax.ShapeDtypeStruct(q.shape, bf16),
-        in_specs=[hbm] * 7,
+        in_specs=[hbm] * 6,
         out_specs=vmem,
         scratch_shapes=[
             pltpu.VMEM((rows, HEAD_DIM), bf16),
             pltpu.VMEM((per_view, BLOCK, HEAD_DIM), bf16),
             pltpu.VMEM((per_view, BLOCK, HEAD_DIM), bf16),
             pltpu.VMEM((2, 1, HEAD_DIM), f32),
+            pltpu.VMEM((TOPK, per_view), jnp.int32),
             pltpu.VMEM((views, 1, HEAD_DIM), jnp.int32),
+            pltpu.VMEM((TOPK, HEAD_DIM), jnp.int32),
             pltpu.SMEM((TOPK, HEAD_DIM), jnp.int32),
             pltpu.VMEM((views, 1, HEAD_DIM), jnp.int32),
             pltpu.SMEM((views, 1, HEAD_DIM), jnp.int32),
@@ -475,14 +475,13 @@
             dma((parts, partners)),
         ],
         compiler_params=pltpu.CompilerParams(
-            collective_id=0, has_side_effects=True, vmem_limit_bytes=56 * 1024 * 1024
+            collective_id=0, has_side_effects=True, vmem_limit_bytes=53 * 1024 * 1024
         ),
     )(
         q,
         k.reshape(per_view, BLOCK, HEAD_DIM),
         v.reshape(per_view, BLOCK, HEAD_DIM),
-        plan,
-        place,
+        lists.T,
         gain_s[None],
         gain_l[None],
     )

time: 136 us -> 132 us (0.971)
  the two profiles are of different devices: /device:TPU:384 before, /device:TPU:352 now
where the time goes in v4:
time: 132 us; the launch traced here: 131 us
  Pallas kernels  130 us (98%)
  local copies, waits for them, and re-layouts  1.48 us (1%)
    pallas_call x1, Pallas kernels, shards(): pl.pallas_call(functools.partial(kernel, views, heads, splits, rows), out...  130 us

profile of v4, /device:TPU:352, one launch (start us, length us, event | category | flops | bytes accessed | tf_op | source)
XLA Modules:
  0.0 131.4 jit_solution(7965803005893065271)
XLA Ops:
  0.0 0.0 copy-start
  0.0 0.0 copy-start.1
  0.0 0.0 copy-start.2
  0.0 0.7 copy-done
  0.7 0.0 copy-done.1
  0.7 0.0 copy-done.2
  0.7 129.9 %shard_map.64 = bf16[2048,128]{1,0:T(8,128)(2,1)S(1)} custom-call(bf16[2048,128]{1,0:T(8,128)(2,1)} %q_hbm.1, bf16[32,64,128]{2,1,0:T(8,128)(2,1)} %bitcast.8, bf16[32,64,128]{2,1,0:T(8,128)(2,1)} %bitcast.9, s32[4,32]{1,0:T(4,128)S(1)} %bitcast.5, f32[1,128]{1,0:T(1,128)S(1)} %bitcast.6, f32[1,128]{1,0:T(1,128)S(1)} %bitcast.7), custom_call_target="tpu_custom_call" | custom-call | tf_op jit(solution)/shard_map/pallas_call | solution.py:433
  130.6 0.8 copy.8
Async XLA Ops:
  0.0 0.7 copy-start
  0.0 0.7 copy-start.1
  0.0 0.7 copy-start.2

commit v5 on v4

--- a/solution.py
+++ b/solution.py
@@ -222,14 +222,22 @@
             device_id_type=MESH,
         )
 
-    for w in send_order(views):
-        @pl.when(w > me)
+    half = views // 2
+
+    def send_blocks(w, when):
+        @pl.when(when)
         def _():
             for s in range(CAP):
                 block = plan_smem[w, 0, s]
                 stage[w * CAP + s, 0] = k_ref[block]
                 stage[w * CAP + s, 1] = v_ref[block]
             bulk_copy(me, w).start()
+
+    def first(w):
+        return half < w < half + 7
+
+    for w in send_order(views):
+        send_blocks(w, (w > me) & ((me >= half) | first(w)))
 
     row = lax.broadcasted_iota(jnp.int32, (qtile, qtile), 0)
     col = lax.broadcasted_iota(jnp.int32, (qtile, qtile), 1)
@@ -268,6 +276,10 @@
         acc[mine, :] = o
         top[mine, :] = jnp.broadcast_to(m, (qtile, HEAD_DIM))
         total[mine, :] = jnp.broadcast_to(l, (qtile, HEAD_DIM))
+
+    for w in send_order(views):
+        if not first(w):
+            send_blocks(w, (w > me) & (me < half))
 
     @pl.when(member < group - 1)
     def _():

time: 132 us -> 128 us (0.970)
  the two profiles are of different devices: /device:TPU:352 before, /device:TPU:480 now
where the time goes in v5:
time: 128 us
  Pallas kernels  126 us (98%)
  local copies, waits for them, and re-layouts  1.48 us (1%)
    pallas_call x1, Pallas kernels, shards(): pl.pallas_call(functools.partial(kernel, views, heads, splits, rows), out...  126 us

profile of v5, /device:TPU:480, one launch (start us, length us, event | category | flops | bytes accessed | tf_op | source)
XLA Modules:
  0.0 127.6 jit_solution(9848579590776321492)
XLA Ops:
  0.0 0.0 copy-start
  0.0 0.0 copy-start.1
  0.0 0.0 copy-start.2
  0.0 0.7 copy-done
  0.7 0.0 copy-done.1
  0.7 0.0 copy-done.2
  0.7 126.2 %shard_map.64 = bf16[2048,128]{1,0:T(8,128)(2,1)S(1)} custom-call(bf16[2048,128]{1,0:T(8,128)(2,1)} %q_hbm.1, bf16[32,64,128]{2,1,0:T(8,128)(2,1)} %bitcast.8, bf16[32,64,128]{2,1,0:T(8,128)(2,1)} %bitcast.9, s32[4,32]{1,0:T(4,128)S(1)} %bitcast.5, f32[1,128]{1,0:T(1,128)S(1)} %bitcast.6, f32[1,128]{1,0:T(1,128)S(1)} %bitcast.7), custom_call_target="tpu_custom_call" | custom-call | tf_op jit(solution)/shard_map/pallas_call | solution.py:445
  126.9 0.8 copy.8
Async XLA Ops:
  0.0 0.7 copy-start
  0.0 0.7 copy-start.1
  0.0 0.7 copy-start.2

commit v6 on v5

--- a/solution.py
+++ b/solution.py
@@ -328,7 +328,7 @@
         )
         return (acc[mine, :] * fade + o) / l, jnp.concatenate(linear, axis=0)
 
-    parts = 4
+    parts = 2
     seg = rows // parts
     chunk = min(seg, HEAD_DIM)
     chunks = seg // chunk
@@ -439,7 +439,7 @@
     vmem = pl.BlockSpec(memory_space=pltpu.VMEM)
     hbm = pl.BlockSpec(memory_space=pltpu.HBM)
     dma = pltpu.SemaphoreType.DMA
-    parts = 4
+    parts = 2
     chunk = min(rows // parts, HEAD_DIM)
     sums = (2 * (rows // parts // chunk), chunk)
     return pl.pallas_call(

time: 128 us -> 127 us (level)
  no operation moved by 1% of the time
where the time goes in v6:
time: 127 us
  Pallas kernels  125 us (98%)
  local copies, waits for them, and re-layouts  1.48 us (1%)
    pallas_call x1, Pallas kernels, shards(): pl.pallas_call(functools.partial(kernel, views, heads, splits, rows), out...  125 us

profile of v6, /device:TPU:480, one launch (start us, length us, event | category | flops | bytes accessed | tf_op | source)
XLA Modules:
  0.0 126.6 jit_solution(1790081222425116351)
XLA Ops:
  0.0 0.0 copy-start
  0.0 0.0 copy-start.1
  0.0 0.0 copy-start.2
  0.0 0.7 copy-done
  0.7 0.0 copy-done.1
  0.7 0.0 copy-done.2
  0.7 125.1 %shard_map.64 = bf16[2048,128]{1,0:T(8,128)(2,1)S(1)} custom-call(bf16[2048,128]{1,0:T(8,128)(2,1)} %q_hbm.1, bf16[32,64,128]{2,1,0:T(8,128)(2,1)} %bitcast.8, bf16[32,64,128]{2,1,0:T(8,128)(2,1)} %bitcast.9, s32[4,32]{1,0:T(4,128)S(1)} %bitcast.5, f32[1,128]{1,0:T(1,128)S(1)} %bitcast.6, f32[1,128]{1,0:T(1,128)S(1)} %bitcast.7), custom_call_target="tpu_custom_call" | custom-call | tf_op jit(solution)/shard_map/pallas_call | solution.py:445
  125.8 0.8 copy.8
Async XLA Ops:
  0.0 0.7 copy-start
  0.0 0.7 copy-start.1
  0.0 0.7 copy-start.2
